TPU v7x, 32 devices: a whole 2x2x4 slice. The times are simulated.
32 devices in a mesh: groups: 2 (over y), cluster: 4 (over x, core), expert: 4 (over z).
Axes of the slice: x: 2, y: 2, z: 4, core: 2. Of those that a mesh axis runs over, the one named last changes fastest.
Arguments:
- tokens: bfloat16 [2048, 2048], P(('groups', 'cluster', 'expert')), parts along dimension 0, may hold values from -6 to 6
- cluster_ids: int32 [2048], P(('groups', 'cluster', 'expert')), parts along dimension 0, may hold values from 0 to 3, as said below
- expert_ids: int32 [2048, 2], P(('groups', 'cluster', 'expert')), parts along dimension 0, may hold values from 0 to 1, as said below
- gate_probs: bfloat16 [2048, 2], P(('groups', 'cluster', 'expert')), parts along dimension 0, may hold values from 0.19921875 to 1
- w_gate: bfloat16 [16, 2048, 384], P(('cluster', 'expert')), may hold values from -0.125 to 0.125
- w_up: bfloat16 [16, 2048, 384], P(('cluster', 'expert')), may hold values from -0.125 to 0.125
- w_down: bfloat16 [16, 384, 2048], P(('cluster', 'expert')), may hold values from -0.21875 to 0.21875
Outputs:
- mixed: bfloat16 [2048, 2048], P(('groups', 'cluster', 'expert')), parts along dimension 0
There are 2 independent parts, one for each index of `groups`. A program takes and returns all parts, laid end to end along the dimension named above; an argument that names none is the same for every part. Nothing has to cross between parts.
Inputs may be any that keep to these rules, and one draw needn't show every extreme that they name: `cluster_ids`: among the tokens of one device (an aligned block of 64 tokens) at most 32 name the same cluster; in every draw some device has exactly 32 tokens of one cluster. `expert_ids`: A token's two expert numbers differ. Among the tokens of one device at most 32 name the same expert number of the same cluster; in every draw some device reaches 32.
All inputs are finite; a program needn't handle non-finite values.
Results may differ from a plain program's by a relative error of at most 0.0059.
Values may be sent and summed in bfloat16 or wider, within the bound.
A program may use at most 64 MiB of HBM per device.

v0:
```python
import jax
import jax.numpy as jnp
from jax import lax
from jax.sharding import PartitionSpec as P


def shards(tokens, cluster_ids, expert_ids, gate_probs, w_gate, w_up, w_down):
    clusters = lax.axis_size("cluster")
    expert_devs = lax.axis_size("expert")
    per_cluster = expert_devs // 2
    tok_count, feat_dim = tokens.shape
    cap_first = 2 * tok_count // clusters
    cap_second = 2 * cap_first // per_cluster
    stride = clusters * cap_second
    own_cluster = lax.axis_index("cluster")
    pair_key = (cluster_ids[:, None] * per_cluster + expert_ids).reshape(-1)
    pair_pos = jnp.arange(2 * tok_count)
    pair_earlier = (pair_key[:, None] == pair_key[None, :]) & (
        pair_pos[None, :] < pair_pos[:, None]
    )
    pair_slot = jnp.sum(pair_earlier.astype(jnp.int32), axis=1).reshape(tok_count, 2)
    tok_pos = jnp.arange(tok_count)
    tok_earlier = (cluster_ids[:, None] == cluster_ids[None, :]) & (
        tok_pos[None, :] < tok_pos[:, None]
    )
    tok_rank = jnp.sum(tok_earlier.astype(jnp.int32), axis=1)
    first_slot = cluster_ids * cap_first + tok_rank
    target = expert_ids * stride + own_cluster * cap_second + pair_slot
    out_rows = jnp.zeros((clusters * cap_first, feat_dim), jnp.bfloat16).at[first_slot].set(tokens)
    out_target = (
        jnp.full((clusters * cap_first, 2), per_cluster * stride, jnp.int32)
        .at[first_slot]
        .set(target)
    )
    out_gates = jnp.zeros((clusters * cap_first, 2), jnp.bfloat16).at[first_slot].set(gate_probs)
    rows_in, target_in, gates_in = (
        lax.all_to_all(
            out_rows.reshape(clusters, cap_first, feat_dim),
            "cluster",
            split_axis=0,
            concat_axis=0,
            tiled=True,
        ),
        lax.all_to_all(
            out_target.reshape(clusters, cap_first, 2),
            "cluster",
            split_axis=0,
            concat_axis=0,
            tiled=True,
        ),
        lax.all_to_all(
            out_gates.reshape(clusters, cap_first, 2),
            "cluster",
            split_axis=0,
            concat_axis=0,
            tiled=True,
        ),
    )
    flat_rows = rows_in.reshape(-1, feat_dim)
    flat_target = target_in.reshape(-1, 2)
    flat_gates = gates_in.reshape(-1, 2).astype(jnp.float32)
    sectioned = jnp.zeros((per_cluster * stride, feat_dim), jnp.bfloat16)
    sectioned = sectioned.at[flat_target[:, 0]].set(flat_rows, mode="drop")
    sectioned = sectioned.at[flat_target[:, 1]].set(flat_rows, mode="drop")
    sectioned = sectioned.reshape(per_cluster, clusters, cap_second, feat_dim)
    gate_half = w_gate[0]
    up_half = w_up[0]
    down_half = w_down[0]
    send = jnp.repeat(sectioned, 2, axis=0)
    block = lax.all_to_all(send, "expert", split_axis=0, concat_axis=2, tiled=True)
    items = block.shape[1]
    rows = block.reshape(-1, feat_dim)
    gate = jnp.dot(rows, gate_half, preferred_element_type=jnp.float32)
    up_part = jnp.dot(rows, up_half, preferred_element_type=jnp.float32)
    hidden = (jax.nn.silu(gate) * up_part).astype(jnp.bfloat16)
    partial_value = jnp.dot(hidden, down_half, preferred_element_type=jnp.float32).reshape(
        1, items, expert_devs * cap_second, feat_dim
    )
    back = lax.all_to_all(partial_value, "expert", split_axis=2, concat_axis=0, tiled=True)
    summed = jnp.sum(back.reshape(per_cluster, 2, items, cap_second, feat_dim), axis=1)
    expert_out = summed.astype(jnp.bfloat16)
    flat_out = expert_out.reshape(-1, feat_dim)
    safe_target = jnp.minimum(flat_target, per_cluster * stride - 1)
    picked = flat_out[safe_target]
    combined = (
        picked[:, 0].astype(jnp.float32) * flat_gates[:, 0:1]
        + picked[:, 1].astype(jnp.float32) * flat_gates[:, 1:2]
    )
    combined = combined.astype(jnp.bfloat16).reshape(clusters, cap_first, feat_dim)
    back_rows = lax.all_to_all(combined, "cluster", split_axis=0, concat_axis=0, tiled=True)
    return back_rows.reshape(-1, feat_dim)[first_slot]


def solution(mesh):
    in_specs = (
        P(("groups", "cluster", "expert"), None),
        P(("groups", "cluster", "expert")),
        P(("groups", "cluster", "expert"), None),
        P(("groups", "cluster", "expert"), None),
        P(("cluster", "expert"), None, None),
        P(("cluster", "expert"), None, None),
        P(("cluster", "expert"), None, None),
    )
    out_specs = P(("groups", "cluster", "expert"), None)
    return jax.shard_map(shards, mesh=mesh, in_specs=in_specs, out_specs=out_specs, check_vma=False)
```

profile of v0, /device:TPU:0, one launch (start us, length us, event | category | flops | bytes accessed | tf_op | source)
XLA Modules:
  0.0 223.0 jit_solution(3265366219179684321)
XLA Ops:
  0.0 0.0 copy-start
  0.0 1.0 convert_reduce_fusion.1
  1.0 0.7 broadcast_multiply_fusion
  1.6 0.7 broadcast_add_fusion
  2.3 0.1 copy.68
  2.4 0.1 eq.31
  2.6 0.2 convert_reduce_fusion
  2.7 0.1 reshape.92
  2.9 0.1 copy.69
  3.0 0.7 add_add_fusion
  3.7 0.1 copy.70
  3.8 0.8 scatter_custom_fusion
  4.5 0.7 copy.71
  5.2 4.2 %all-to-all-start = ((s32[4,32,2]{1,2,0:T(2,128)}), s32[4,32,2]{1,2,0:T(2,128)S(1)}, u32[]{:S(2)}, u32[]{:S(2)}) async-start(s32[4,32,2]{1,2,0:T(2,128)} %copy.71), calls=%async_computation | async-start | bytes 8192 | tf_op jit(solution)/shard_map/all_to_all | solution.py:44
  9.4 2.2 scatter_custom_fusion.1
  11.6 1.6 all-to-all-done
  13.2 3.5 %all-to-all-start.1 = ((bf16[4,32,2048]{2,1,0:T(8,128)(2,1)}), bf16[4,32,2048]{2,1,0:T(8,128)(2,1)S(1)}, u32[]{:S(2)}, u32[]{:S(2)}) async-start(bf16[4,32,2048]{2,1,0:T(8,128)(2,1)} %bitcast.2), calls=%async_computation.1 | async-start | bytes 1048576 | tf_op jit(solution)/shard_map/all_to_all | solution.py:37
  16.7 0.1 reshape.94
  16.8 8.7 %all-to-all-done.1 = bf16[4,32,2048]{2,1,0:T(8,128)(2,1)S(1)} async-done(((bf16[4,32,2048]{2,1,0:T(8,128)(2,1)}), bf16[4,32,2048]{2,1,0:T(8,128)(2,1)S(1)}, u32[]{:S(2)}, u32[]{:S(2)}) %all-to-all-start.1) | async-done | bytes 524320 | tf_op jit(solution)/shard_map/all_to_all | solution.py:37
  25.5 1.7 scatter_custom_fusion.2
  27.2 1.9 scatter_fusion
  29.1 1.5 broadcast_in_dim.13
  30.7 0.0 copy-start.1
  30.7 5.5 %all-to-all-start.2 = ((bf16[4,4,32,2048]{3,2,1,0:T(8,128)(2,1)}), bf16[4,4,32,2048]{3,2,1,0:T(8,128)(2,1)}, u32[]{:S(2)}, u32[]{:S(2)}) async-start(bf16[4,4,32,2048]{3,2,1,0:T(8,128)(2,1)} %bitcast.59), calls=%async_computation.2 | async-start | bytes 4194304 | tf_op jit(solution)/shard_map/all_to_all | solution.py:70
  36.2 0.0 copy-done.1
  36.2 0.1 copy.79
  36.3 0.8 scatter_custom_fusion.4
  37.0 0.7 copy.80
  37.7 46.5 %all-to-all-done.2 = bf16[4,4,32,2048]{3,2,1,0:T(8,128)(2,1)} async-done(((bf16[4,4,32,2048]{3,2,1,0:T(8,128)(2,1)}), bf16[4,4,32,2048]{3,2,1,0:T(8,128)(2,1)}, u32[]{:S(2)}, u32[]{:S(2)}) %all-to-all-start.2) | async-done | bytes 2097184 | tf_op jit(solution)/shard_map/all_to_all | solution.py:70
  84.3 3.2 %all-to-all-start.4 = ((bf16[4,32,2]{1,2,0:T(2,128)(2,1)}), bf16[4,32,2]{1,2,0:T(2,128)(2,1)S(1)}, u32[]{:S(2)}, u32[]{:S(2)}) async-start(bf16[4,32,2]{1,2,0:T(2,128)(2,1)} %copy.80), calls=%async_computation.4 | async-start | bytes 4096 | tf_op jit(solution)/shard_map/all_to_all | solution.py:51
  87.5 0.0 copy-start.2
  87.5 1.8 copy.73
  89.4 0.2 copy-done.2
  89.5 0.0 copy-start.3
  89.5 1.2 fusion.3
  90.8 0.2 copy-done.3
  90.9 1.3 fusion.8
  92.2 0.0 copy-done
  92.2 1.3 convolution_bitcast_fusion
  93.5 4.7 %copy.74 = f32[1,4,128,2048]{3,1,0,2:T(4,128)} copy(f32[1,4,128,2048]{3,2,1,0:T(8,128)S(1)} %convolution_bitcast_fusion) | data formatting | bytes 8388608 | tf_op jit(solution)/shard_map/dot_general | solution.py:76
  98.2 0.0 all-to-all-done.4
  98.2 5.0 %all-to-all-start.3 = ((f32[1,4,128,2048]{3,1,0,2:T(4,128)}), f32[1,4,128,2048]{3,1,0,2:T(4,128)}, u32[]{:S(2)}, u32[]{:S(2)}) async-start(f32[1,4,128,2048]{3,1,0,2:T(4,128)} %copy.74), calls=%async_computation.3 | async-start | bytes 8388608 | tf_op jit(solution)/shard_map/all_to_all | solution.py:79
  103.2 0.1 reshape.105
  103.4 0.1 mul.60
  103.4 0.1 mul.63
  103.5 0.1 min.18
  103.6 0.1 copy.78
  103.7 0.1 reshape.109
  103.9 93.3 %all-to-all-done.3 = f32[1,4,128,2048]{3,1,0,2:T(4,128)} async-done(((f32[1,4,128,2048]{3,1,0,2:T(4,128)}), f32[1,4,128,2048]{3,1,0,2:T(4,128)}, u32[]{:S(2)}, u32[]{:S(2)}) %all-to-all-start.3) | async-done | bytes 4194336 | tf_op jit(solution)/shard_map/all_to_all | solution.py:79
  197.2 4.2 %reduce = bf16[2,1,4,32,2048]{4,2,3,0,1:T(4,128)(2,1)S(1)} reduce(f32[2,2,1,4,32,2048]{5,3,4,1,0,2:T(4,128)} %bitcast.21, f32[]{:T(128)} %constant.5.clone.1), dimensions={1}, to_apply=%region_6.0 | reduce | flops 524288 | bytes 5242884
  201.4 0.6 copy.89
  201.9 0.1 copy.76
  202.0 2.4 %gather_fusion = bf16[256,2048]{1,0:T(8,128)(2,1)} fusion(bf16[256,2048]{1,0:T(8,128)(2,1)S(1)} %bitcast.56, s32[1024]{0:T(1024)S(1)} %pad_clamp_fusion.1), kind=kCustom, calls=%fused_computation | custom fusion | bytes 2098176 | tf_op jit(solution)/shard_map/gather | solution.py:84
  204.4 1.7 reshape.108
  206.1 1.4 slice_convert_fusion.1
  207.6 0.3 copy.83
  207.9 0.3 copy.84
  208.3 1.0 add_convert_fusion
  209.3 3.5 %all-to-all-start.5 = ((bf16[4,32,2048]{2,1,0:T(8,128)(2,1)}), bf16[4,32,2048]{2,1,0:T(8,128)(2,1)S(1)}, u32[]{:S(2)}, u32[]{:S(2)}) async-start(bf16[4,32,2048]{2,1,0:T(8,128)(2,1)} %add_convert_fusion), calls=%async_computation.5 | async-start | bytes 1048576 | tf_op jit(solution)/shard_map/all_to_all | solution.py:90
  212.8 8.8 %all-to-all-done.5 = bf16[4,32,2048]{2,1,0:T(8,128)(2,1)S(1)} async-done(((bf16[4,32,2048]{2,1,0:T(8,128)(2,1)}), bf16[4,32,2048]{2,1,0:T(8,128)(2,1)S(1)}, u32[]{:S(2)}, u32[]{:S(2)}) %all-to-all-start.5) | async-done | bytes 524320 | tf_op jit(solution)/shard_map/all_to_all | solution.py:90
  221.6 1.4 gather_fusion.1
  (7 shorter events, 0.1 us)
Async XLA Ops:
  0.0 92.2 %copy-start = (bf16[1,384,2048]{2,1,0:T(8,128)(2,1)S(1)}, bf16[1,384,2048]{2,1,0:T(8,128)(2,1)}, u32[]{:S(2)}) copy-start(bf16[1,384,2048]{2,1,0:T(8,128)(2,1)} %param.13) | copy-start | bytes 4718596
  5.2 8.0 %all-to-all-start = ((s32[4,32,2]{1,2,0:T(2,128)}), s32[4,32,2]{1,2,0:T(2,128)S(1)}, u32[]{:S(2)}, u32[]{:S(2)}) async-start(s32[4,32,2]{1,2,0:T(2,128)} %copy.71), calls=%async_computation | async-start | bytes 8192 | tf_op jit(solution)/shard_map/all_to_all | solution.py:44
  13.2 12.3 %all-to-all-start.1 = ((bf16[4,32,2048]{2,1,0:T(8,128)(2,1)}), bf16[4,32,2048]{2,1,0:T(8,128)(2,1)S(1)}, u32[]{:S(2)}, u32[]{:S(2)}) async-start(bf16[4,32,2048]{2,1,0:T(8,128)(2,1)} %bitcast.2), calls=%async_computation.1 | async-start | bytes 1048576 | tf_op jit(solution)/shard_map/all_to_all | solution.py:37
  30.7 5.5 %copy-start.1 = (bf16[64,2]{0,1:T(2,128)(2,1)S(1)}, bf16[64,2]{0,1:T(2,128)(2,1)}, u32[]{:S(2)}) copy-start(bf16[64,2]{0,1:T(2,128)(2,1)} %param.10) | copy-start | bytes 772
  30.7 53.6 %all-to-all-start.2 = ((bf16[4,4,32,2048]{3,2,1,0:T(8,128)(2,1)}), bf16[4,4,32,2048]{3,2,1,0:T(8,128)(2,1)}, u32[]{:S(2)}, u32[]{:S(2)}) async-start(bf16[4,4,32,2048]{3,2,1,0:T(8,128)(2,1)} %bitcast.59), calls=%async_computation.2 | async-start | bytes 4194304 | tf_op jit(solution)/shard_map/all_to_all | solution.py:70
  84.3 13.9 %all-to-all-start.4 = ((bf16[4,32,2]{1,2,0:T(2,128)(2,1)}), bf16[4,32,2]{1,2,0:T(2,128)(2,1)S(1)}, u32[]{:S(2)}, u32[]{:S(2)}) async-start(bf16[4,32,2]{1,2,0:T(2,128)(2,1)} %copy.80), calls=%async_computation.4 | async-start | bytes 4096 | tf_op jit(solution)/shard_map/all_to_all | solution.py:51
  87.5 2.0 copy-start.2
  89.5 1.4 copy-start.3
  98.2 99.0 %all-to-all-start.3 = ((f32[1,4,128,2048]{3,1,0,2:T(4,128)}), f32[1,4,128,2048]{3,1,0,2:T(4,128)}, u32[]{:S(2)}, u32[]{:S(2)}) async-start(f32[1,4,128,2048]{3,1,0,2:T(4,128)} %copy.74), calls=%async_computation.3 | async-start | bytes 8388608 | tf_op jit(solution)/shard_map/all_to_all | solution.py:79
  209.3 12.3 %all-to-all-start.5 = ((bf16[4,32,2048]{2,1,0:T(8,128)(2,1)}), bf16[4,32,2048]{2,1,0:T(8,128)(2,1)S(1)}, u32[]{:S(2)}, u32[]{:S(2)}) async-start(bf16[4,32,2048]{2,1,0:T(8,128)(2,1)} %add_convert_fusion), calls=%async_computation.5 | async-start | bytes 1048576 | tf_op jit(solution)/shard_map/all_to_all | solution.py:90
where the time goes:
time: 224 us; the launch traced here: 223 us
  waiting for transfers between devices  159 us (71%)
  local copies, waits for them, and re-layouts  25.4 us (11%)
  starting transfers between devices  24.9 us (11%)
  other arithmetic  9.84 us (4%)
  matrix products  3.8 us (2%)
    all_to_all x1, waiting for transfers between devices, shards(): lax.all_to_all(partial_value, 'expert', split_axis=2, concat_axis=0, tile...  93.3 us
    all_to_all x1, waiting for transfers between devices, shards(): lax.all_to_all(send, 'expert', split_axis=0, concat_axis=2, tiled=True)  46.5 us
    all_to_all x1, waiting for transfers between devices, shards(): lax.all_to_all(combined, 'cluster', split_axis=0, concat_axis=0, tiled=True)  8.8 us
    all_to_all x1, waiting for transfers between devices, shards(): lax.all_to_all(out_rows.reshape(clusters, cap_first, feat_dim), 'cluster'...  8.71 us
    all_to_all x1, starting transfers between devices, shards(): lax.all_to_all(send, 'expert', split_axis=0, concat_axis=2, tiled=True)  5.46 us
    all_to_all x1, starting transfers between devices, shards(): lax.all_to_all(partial_value, 'expert', split_axis=2, concat_axis=0, tile...  5.04 us
    dot_general x1, local copies, waits for them, and re-layouts, shards(): jnp.dot(hidden, down_half, preferred_element_type=jnp.float32)  4.67 us
  transfers between devices with their start and end apart: 6, of which 5 were waited for; matrix products, arithmetic and copies ran while one was open for 7% of the time, Pallas kernels for 0%

commit v1 on v0

--- a/solution.py
+++ b/solution.py
@@ -4,7 +4,7 @@
 from jax.sharding import PartitionSpec as P
 
 
-def shards(tokens, cluster_ids, expert_ids, gate_probs, w_gate, w_up, w_down):
+def routed(tokens, cluster_ids, expert_ids, gate_probs, w_gate, w_up, w_down):
     clusters = lax.axis_size("cluster")
     expert_devs = lax.axis_size("expert")
     per_cluster = expert_devs // 2
@@ -91,7 +91,24 @@
     return back_rows.reshape(-1, feat_dim)[first_slot]
 
 
+def dense(tokens, cluster_ids, expert_ids, gate_probs, w_gate, w_up, w_down):
+    axes = ("cluster", "expert")
+    own_expert = lax.axis_index("cluster") * 2 + lax.axis_index("expert") // 2
+    rows = lax.all_gather(tokens, axes, axis=0, tiled=True)
+    wanted = jnp.arange(8) == cluster_ids[:, None, None] * 2 + expert_ids[:, :, None]
+    table = jnp.sum(jnp.where(wanted, gate_probs.astype(jnp.float32)[:, :, None], 0.0), axis=1)
+    table = lax.all_gather(table.T, axes, axis=1, tiled=True)
+    weight = lax.dynamic_index_in_dim(table, own_expert, 0, keepdims=False)
+    gate = jnp.dot(rows, w_gate[0], preferred_element_type=jnp.float32)
+    up_part = jnp.dot(rows, w_up[0], preferred_element_type=jnp.float32)
+    hidden = (jax.nn.silu(gate) * up_part).astype(jnp.bfloat16)
+    partial = jnp.dot(hidden, w_down[0], preferred_element_type=jnp.float32)
+    partial = (partial * weight[:, None]).astype(jnp.bfloat16)
+    return lax.psum_scatter(partial, axes, scatter_dimension=0, tiled=True)
+
+
 def solution(mesh):
+    shards = dense if mesh.shape["expert"] == 4 else routed
     in_specs = (
         P(("groups", "cluster", "expert"), None),
         P(("groups", "cluster", "expert")),

time: 224 us -> 156 us (0.70)
  waiting for transfers between devices: 159 us -> 91 us
  blocking collectives: 0 us -> 34.8 us
  local copies, waits for them, and re-layouts: 25.4 us -> 0.12 us
  starting transfers between devices: 24.9 us -> 0.04 us
  between operations: 0.22 us -> 13.4 us
  matrix products: 3.8 us -> 14.1 us
  other arithmetic: 9.84 us -> 2 us
    all_to_all x6 -> x0, waiting for transfers between devices: 159 us -> none  [the longest x1 93.3 us: shards(): lax.all_to_all(partial_value, 'expert', split_axis=2, concat_axis=0, tile...]
    reduce_scatter x0 -> x1, waiting for transfers between devices: none -> 71.3 us  [dense(): return lax.psum_scatter(partial, axes, scatter_dimension=0, tiled=True)]
    all_gather x0 -> x1, blocking collectives: none -> 34.8 us  [dense(): table = lax.all_gather(table.T, axes, axis=1, tiled=True)]
    all_to_all x6 -> x0, starting transfers between devices: 24.9 us -> none  [the longest x1 5.46 us: shards(): lax.all_to_all(send, 'expert', split_axis=0, concat_axis=2, tiled=True)]
    all_gather x0 -> x1, waiting for transfers between devices: none -> 19 us  [dense(): rows = lax.all_gather(tokens, axes, axis=0, tiled=True)]
    dot_general x3 -> x2, matrix products: 3.8 us -> 14.1 us  [the longest x1 7.85 us: dense(): partial = jnp.dot(hidden, w_down[0], preferred_element_type=jnp.float32)]
    scatter x5 -> x0, local copies, waits for them, and re-layouts: 7.36 us -> none  [the longest x1 2.21 us: shards(): jnp.zeros((clusters * cap_first, feat_dim), jnp.bfloat16).at[first_slot]]
    gather x3 -> x0, local copies, waits for them, and re-layouts: 5.54 us -> none  [the longest x2 4.1 us: shards(): picked = flat_out[safe_target]]
  transfers between devices with their start and end apart: 6 -> 2, of which waited for: 5 -> 2; matrix products, arithmetic and copies ran while one was open for 7% -> 1% of each run, Pallas kernels for 0% -> 0%
where the time goes in v1:
time: 156 us; the launch traced here: 155 us
  waiting for transfers between devices  91 us (58%)
  blocking collectives  34.8 us (22%)
  matrix products  14.1 us (9%)
  between operations  13.4 us (9%)
  other arithmetic  2 us (1%)
    reduce_scatter x1, waiting for transfers between devices, dense(): return lax.psum_scatter(partial, axes, scatter_dimension=0, tiled=True)  71.3 us
    all_gather x1, blocking collectives, dense(): table = lax.all_gather(table.T, axes, axis=1, tiled=True)  34.8 us
    all_gather x1, waiting for transfers between devices, dense(): rows = lax.all_gather(tokens, axes, axis=0, tiled=True)  19 us
    dot_general x1, matrix products, dense(): partial = jnp.dot(hidden, w_down[0], preferred_element_type=jnp.float32)  7.85 us
    dot_general x1, matrix products, dense(): gate = jnp.dot(rows, w_gate[0], preferred_element_type=jnp.float32)  6.23 us
  transfers between devices with their start and end apart: 2, of which 2 were waited for; matrix products, arithmetic and copies ran while one was open for 1% of the time, Pallas kernels for 0%

profile of v1, /device:TPU:0, one launch (start us, length us, event | category | flops | bytes accessed | tf_op | source)
XLA Modules:
  0.0 155.4 jit_solution(6956324145252234887)
XLA Ops:
  6.5 0.0 copy-start
  6.5 0.0 all-gather.3.cloned.1.call-start
  6.5 0.7 all-gather.3.cloned.1.call-update
  7.3 0.0 reduce-scatter.2.cloned.1.call-start
  7.3 0.7 convert_element_type.10
  8.0 0.7 broadcast_multiply_fusion
  8.6 0.7 broadcast_add_fusion
  9.3 34.8 %all-gather = f32[16,64,8]{1,2,0:T(8,128)S(1)} all-gather(f32[1,64,8]{1,2,0:T(8,128)S(1)} %bitcast.19), channel_id=1, replica_groups=mesh['groups'=2,'cluster'=4,'expert'=4] {'cluster','expert'}, dimensions={0}, use_global_device_ids=true | all-gather | bytes 34816 | tf_op jit(solution)/shard_map/all_gather | solution.py:100
  44.1 0.1 reshape.10
  44.2 0.0 copy-start.1
  44.2 19.0 %all-gather.3.cloned.1.call-done = bf16[1024,2048]{1,0:T(8,128)(2,1)} async-done(((bf16[64,2048]{1,0:T(8,128)(2,1)}), bf16[1024,2048]{1,0:T(8,128)(2,1)}) %all-gather.3.cloned.1.call-update) | async-done | bytes 4194320 | tf_op jit(solution)/shard_map/all_gather | solution.py:97
  63.2 6.2 %fusion.3 = f32[1024,384]{1,0:T(8,128)} fusion(bf16[1024,2048]{1,0:T(8,128)(2,1)} %all-gather.3.cloned.1.call-done, bf16[1,2048,384]{2,1,0:T(8,128)(2,1)} %param.11), kind=kOutput, calls=%fused_computation.4 | convolution fusion | flops 1610612736 | bytes 7340032 | tf_op jit(solution)/shard_map/dot_general | solution.py:102
  69.4 0.0 copy-done
  69.4 0.0 copy-done.1
  69.4 7.9 %multiply_convert_fusion = bf16[1024,2048]{1,0:T(8,128)(2,1)} fusion(f32[1024]{0:T(1024)S(1)} %bitcast.20, bf16[1,384,2048]{2,1,0:T(8,128)(2,1)S(1)} %copy-done, f32[1024,384]{1,0:T(8,128)} %fusion.3, bf16[1024,2048]{1,0:T(8,128)(2,1)} %all-gather.3.cloned.1.call-done, bf16[1,2048,384]{2,1,0:T(8,128)(2,1)S(1)} %copy-done.1), kind=kOutput, calls=%fused_computation | convolution fusion | flops 3227779072 | bytes 13111296 | tf_op jit(solution)/shard_map/dot_general | solution.py:105
  77.3 0.0 reduce-scatter.2.cloned.1.call-update
  77.3 71.3 %reduce-scatter.2.cloned.1.call-done = bf16[64,2048]{1,0:T(8,128)(2,1)} async-done(((bf16[1024,2048]{1,0:T(8,128)(2,1)}), bf16[64,2048]{1,0:T(8,128)(2,1)}) %reduce-scatter.2.cloned.1.call-update) | async-done | bytes 262160 | tf_op jit(solution)/shard_map/reduce_scatter | solution.py:107
  (3 shorter events, 0.0 us)
Async XLA Ops:
  6.5 62.9 %copy-start = (bf16[1,384,2048]{2,1,0:T(8,128)(2,1)S(1)}, bf16[1,384,2048]{2,1,0:T(8,128)(2,1)}, u32[]{:S(2)}) copy-start(bf16[1,384,2048]{2,1,0:T(8,128)(2,1)} %param.13) | copy-start | bytes 4718596
  6.5 56.7 %all-gather.3.cloned.1.call-start = ((), (), s32[]{:S(2)}) async-start(), calls=%async_computation.1 | async-start | bytes 4456448 | tf_op jit(solution)/shard_map/all_gather | solution.py:97
  7.3 141.3 %reduce-scatter.2.cloned.1.call-start = ((), (), s32[]{:S(2)}) async-start(), calls=%async_computation.2 | async-start | bytes 4456448 | tf_op jit(solution)/shard_map/reduce_scatter | solution.py:107
  44.2 25.2 %copy-start.1 = (bf16[1,2048,384]{2,1,0:T(8,128)(2,1)S(1)}, bf16[1,2048,384]{2,1,0:T(8,128)(2,1)}, u32[]{:S(2)}) copy-start(bf16[1,2048,384]{2,1,0:T(8,128)(2,1)} %param.12) | copy-start | bytes 4718596
Sparse Core Ops, SparseCore 0:
  9.6 53.5 all-gather.2
  77.4 71.0 reduce-scatter.1

commit v2 on v0

--- a/solution.py
+++ b/solution.py
@@ -1,10 +1,12 @@
 import jax
 import jax.numpy as jnp
 from jax import lax
+from jax.experimental import pallas as pl
+from jax.experimental.pallas import tpu as pltpu
 from jax.sharding import PartitionSpec as P
 
 
-def shards(tokens, cluster_ids, expert_ids, gate_probs, w_gate, w_up, w_down):
+def routed(tokens, cluster_ids, expert_ids, gate_probs, w_gate, w_up, w_down):
     clusters = lax.axis_size("cluster")
     expert_devs = lax.axis_size("expert")
     per_cluster = expert_devs // 2
@@ -91,7 +93,271 @@
     return back_rows.reshape(-1, feat_dim)[first_slot]
 
 
+MESH = pl.DeviceIdType.MESH
+LANES = 128
+
+
+def layer_kernel(
+    tok_ref, table_ref, wg_hbm, wu_hbm, wd_hbm, out_ref,
+    rows, part, core_in, x_in, z_in, wg, wu, wd,
+    w_sem, zs, zr, xs, xr, ss, sr, ps, pr, bs, br, cs, cr,
+):
+    group = lax.axis_index("groups")
+    c = lax.axis_index("cluster")
+    z = lax.axis_index("expert")
+    count, feat = tok_ref.shape
+    depth = 4
+    twin = (group, c + 1 - 2 * (c % 2), z)
+    across = (group, (c + 2) % 4, z)
+    below, above = (group, c, z - 1), (group, c, z + 1)
+    own_expert = c * 2 + z // 2
+
+    loads = [
+        pltpu.make_async_copy(src.at[0], dst, w_sem.at[i])
+        for i, (src, dst) in enumerate(((wg_hbm, wg), (wu_hbm, wu), (wd_hbm, wd)))
+    ]
+    for load in loads:
+        load.start()
+    rows[z, pl.ds(0, count), pl.ds(0, feat)] = tok_ref[...]
+    rows[z, pl.ds(0, count), pl.ds(feat, LANES)] = table_ref[...]
+
+    barrier = pltpu.get_barrier_semaphore()
+    pl.semaphore_signal(barrier, inc=1, device_id=twin, device_id_type=MESH)
+    pl.semaphore_signal(barrier, inc=1, device_id=across, device_id_type=MESH)
+
+    @pl.when(z > 0)
+    def _():
+        pl.semaphore_signal(barrier, inc=1, device_id=below, device_id_type=MESH)
+
+    @pl.when(z < depth - 1)
+    def _():
+        pl.semaphore_signal(barrier, inc=1, device_id=above, device_id_type=MESH)
+
+    middle = (z > 0) & (z < depth - 1)
+    pl.semaphore_wait(barrier, 3 + middle.astype(jnp.int32))
+
+    def remote(src, dst, send, recv, device):
+        return pltpu.make_async_remote_copy(
+            src_ref=src, dst_ref=dst, send_sem=send, recv_sem=recv,
+            device_id=device, device_id_type=MESH,
+        )
+
+    def block(b, r):
+        return rows.at[b, pl.ds(r * count, count)]
+
+    def piece(b, r):
+        return part.at[b, pl.ds(r * count, count)]
+
+    def to_z(b, up):
+        return remote(block(b, 0), block(b, 0), zs.at[up, b], zr.at[b], above if up else below)
+
+    def to_x(b):
+        return remote(block(b, 0), block(b, 2), xs.at[b], xr.at[b], across)
+
+    def to_twin(b, r):
+        i = r // 2
+        return remote(block(b, r), block(b, r + 1), ss.at[i, b], sr.at[i, b], twin)
+
+    def part_to_twin(b, r):
+        i = r // 2
+        return remote(piece(b, r), core_in.at[i, b], ps.at[i, b], pr.at[i, b], twin)
+
+    def part_to_x(b):
+        return remote(piece(b, 2), x_in.at[b], bs.at[b], br.at[b], across)
+
+    def sum_up(b):
+        return remote(piece(b, 0), z_in.at[b], cs.at[b], cr.at[b], above)
+
+    def sum_down(b):
+        last = (b == z - 1).astype(jnp.int32)
+        slot = b * (1 - last) + depth * last
+        return remote(piece(b, 0), z_in.at[slot], cs.at[b], cr.at[slot], below)
+
+    def order(k):
+        far = 3 * (2 - z)
+        inner = jnp.where(k == 0, z, jnp.where(k == 1, z - 1, jnp.where(k == 2, z + 1, far)))
+        return jnp.where(z == 0, k, jnp.where(z == depth - 1, depth - 1 - k, inner))
+
+    def spread(b):
+        to_x(b).start()
+        to_twin(b, 0).start()
+
+    @pl.when(z < depth - 1)
+    def _():
+        to_z(z, 1).start()
+
+    @pl.when(z > 0)
+    def _():
+        to_z(z, 0).start()
+
+    spread(z)
+
+    def fold_core(b):
+        part_to_twin(b, 3).wait_recv()
+        piece(b, 2)[...] = piece(b, 2)[...] + core_in[1, b]
+        part_to_x(b).start()
+
+    def compute(b):
+        lhs = rows[b, :, pl.ds(0, feat)]
+        gate = jnp.dot(lhs, wg[...], preferred_element_type=jnp.float32)
+        up_part = jnp.dot(lhs, wu[...], preferred_element_type=jnp.float32)
+        hidden = (gate / (1.0 + jnp.exp(-gate)) * up_part).astype(jnp.bfloat16)
+        weights = rows[b, :, pl.ds(feat, LANES)].astype(jnp.float32)
+        lane = lax.broadcasted_iota(jnp.int32, weights.shape, 1)
+        weight = jnp.sum(jnp.where(lane == own_expert, weights, 0.0), axis=1, keepdims=True)
+        tile = min(feat, 512)
+        for n in range(feat // tile):
+            cols = pl.ds(n * tile, tile)
+            out = jnp.dot(hidden, wd[:, cols], preferred_element_type=jnp.float32)
+            part[b, :, cols] = (out * weight).astype(jnp.bfloat16)
+
+    def stage(d, carry):
+        for side in (-1, 1):
+            b = z + side * d
+
+            @pl.when((d < depth) & (b >= 0) & (b < depth))
+            def _():
+                to_z(b, 0).wait_recv()
+                if side < 0:
+
+                    @pl.when(z < depth - 1)
+                    def _():
+                        to_z(b, 1).start()
+                else:
+
+                    @pl.when(z > 0)
+                    def _():
+                        to_z(b, 0).start()
+
+                spread(b)
+
+        b = order(d - 1)
+        to_x(b).wait_recv()
+        to_twin(b, 2).start()
+
+        @pl.when(d == depth)
+        def _():
+            fold_core(order(depth - 2))
+
+        @pl.when(d == 1)
+        def _():
+            for load in loads:
+                load.wait()
+
+        to_twin(b, 0).wait_recv()
+        to_twin(b, 2).wait_recv()
+        compute(b)
+        part_to_twin(b, 3).start()
+        part_to_twin(b, 1).start()
+        return carry
+
+    lax.fori_loop(1, depth + 1, stage, 0)
+    for k in (3, 1, 0):
+        fold_core(order(k))
+
+    def total(b):
+        part_to_twin(b, 1).wait_recv()
+        part_to_x(b).wait_recv()
+        value = piece(b, 0)[...].astype(jnp.float32) + core_in[0, b].astype(jnp.float32)
+        return value + x_in[b].astype(jnp.float32)
+
+    def fold(j, carry):
+        b = order(jnp.where(j == 0, 2, jnp.where(j == 1, 3, 1)))
+        piece(b, 0)[...] = total(b).astype(jnp.bfloat16)
+
+        @pl.when(((b > z) & (z > 0)) | ((b < z) & (z < depth - 1)))
+        def _():
+            sum_up(b).wait_recv()
+            mine = piece(b, 0)[...].astype(jnp.float32)
+            piece(b, 0)[...] = (mine + z_in[b].astype(jnp.float32)).astype(jnp.bfloat16)
+
+        @pl.when(b > z)
+        def _():
+            sum_up(b).start()
+
+        @pl.when(b < z)
+        def _():
+            sum_down(b).start()
+
+        return carry
+
+    lax.fori_loop(0, depth - 1, fold, 0)
+    out_ref[...] = total(z).astype(jnp.bfloat16)
+    for slot, there in ((z, z > 0), (depth, z < depth - 1)):
+
+        @pl.when(there)
+        def _():
+            remote(piece(z, 0), z_in.at[slot], cs.at[z], cr.at[slot], across).wait_recv()
+            mine = out_ref[...].astype(jnp.float32)
+            out_ref[...] = (mine + z_in[slot].astype(jnp.float32)).astype(jnp.bfloat16)
+
+    def drain(b, carry):
+        @pl.when((z < depth - 1) & (b <= z))
+        def _():
+            to_z(b, 1).wait_send()
+
+        @pl.when((z > 0) & (b >= z))
+        def _():
+            to_z(b, 0).wait_send()
+
+        to_x(b).wait_send()
+        to_twin(b, 0).wait_send()
+        to_twin(b, 2).wait_send()
+        part_to_twin(b, 1).wait_send()
+        part_to_twin(b, 3).wait_send()
+        part_to_x(b).wait_send()
+
+        @pl.when(b != z)
+        def _():
+            sum_up(b).wait_send()
+
+        return carry
+
+    lax.fori_loop(0, depth, drain, 0)
+
+
+def fused(tokens, cluster_ids, expert_ids, gate_probs, w_gate, w_up, w_down):
+    count, feat = tokens.shape
+    half = w_gate.shape[2]
+    lane = jnp.arange(LANES)
+    pair = cluster_ids[:, None] * 2 + expert_ids
+    table = jnp.where(pair[:, 0:1] == lane, gate_probs[:, 0:1], 0)
+    table = jnp.where(pair[:, 1:2] == lane, gate_probs[:, 1:2], table).astype(jnp.bfloat16)
+    vmem = pl.BlockSpec(memory_space=pltpu.VMEM)
+    hbm = pl.BlockSpec(memory_space=pl.ANY)
+    b16 = jnp.bfloat16
+    dma = pltpu.SemaphoreType.DMA
+    return pl.pallas_call(
+        layer_kernel,
+        out_shape=jax.ShapeDtypeStruct((count, feat), b16),
+        in_specs=[vmem, vmem, hbm, hbm, hbm],
+        out_specs=vmem,
+        scratch_shapes=[
+            pltpu.VMEM((4, 4 * count, feat + LANES), b16),
+            pltpu.VMEM((4, 4 * count, feat), b16),
+            pltpu.VMEM((2, 4, count, feat), b16),
+            pltpu.VMEM((4, count, feat), b16),
+            pltpu.VMEM((5, count, feat), b16),
+            pltpu.VMEM((feat, half), b16),
+            pltpu.VMEM((feat, half), b16),
+            pltpu.VMEM((half, feat), b16),
+            dma((3,)),
+            dma((2, 4)), dma((4,)),
+            dma((4,)), dma((4,)),
+            dma((2, 4)), dma((2, 4)),
+            dma((2, 4)), dma((2, 4)),
+            dma((4,)), dma((4,)),
+            dma((4,)), dma((5,)),
+        ],
+        compiler_params=pltpu.CompilerParams(
+            collective_id=0, has_side_effects=True, vmem_limit_bytes=48 * 2**20
+        ),
+    )(tokens, table, w_gate, w_up, w_down)
+
+
 def solution(mesh):
+    two_of_two = mesh.shape["cluster"] == 4 and mesh.shape["expert"] == 4
+    shards = fused if two_of_two else routed
     in_specs = (
         P(("groups", "cluster", "expert"), None),
         P(("groups", "cluster", "expert")),

time: 224 us -> 79 us (0.35)
  waiting for transfers between devices: 159 us -> 0 us
  Pallas kernels: 0 us -> 70.6 us
  starting transfers between devices: 24.9 us -> 0 us
  local copies, waits for them, and re-layouts: 25.4 us -> 6.61 us
  other arithmetic: 9.84 us -> 1.43 us
  matrix products: 3.8 us -> 0 us
    all_to_all x6 -> x0, waiting for transfers between devices: 159 us -> none  [the longest x1 93.3 us: shards(): lax.all_to_all(partial_value, 'expert', split_axis=2, concat_axis=0, tile...]
    pallas_call x0 -> x1, Pallas kernels: none -> 70.6 us  [fused(): pl.pallas_call(layer_kernel, out_shape=jax.ShapeDtypeStruct((count, feat)...]
    all_to_all x6 -> x0, starting transfers between devices: 24.9 us -> none  [the longest x1 5.46 us: shards(): lax.all_to_all(send, 'expert', split_axis=0, concat_axis=2, tiled=True)]
    scatter x5 -> x0, local copies, waits for them, and re-layouts: 7.36 us -> none  [the longest x1 2.21 us: shards(): jnp.zeros((clusters * cap_first, feat_dim), jnp.bfloat16).at[first_slot]]
    gather x3 -> x0, local copies, waits for them, and re-layouts: 5.54 us -> none  [the longest x2 4.1 us: shards(): picked = flat_out[safe_target]]
    dot_general x1 -> x0, local copies, waits for them, and re-layouts: 4.67 us -> none  [shards(): jnp.dot(hidden, down_half, preferred_element_type=jnp.float32)]
    unnamed x1 -> x0, other arithmetic: 4.19 us -> none
    unnamed x12 -> x9, local copies, waits for them, and re-layouts: 1.72 us -> 5.87 us
  transfers between devices with their start and end apart: 6 -> 0, of which waited for: 5 -> 0; matrix products, arithmetic and copies ran while one was open for 7% -> 0% of each run, Pallas kernels for 0% -> 0%
where the time goes in v2:
time: 79 us; the launch traced here: 78.7 us
  Pallas kernels  70.6 us (89%)
  local copies, waits for them, and re-layouts  6.61 us (8%)
  other arithmetic  1.43 us (2%)
    pallas_call x1, Pallas kernels, fused(): pl.pallas_call(layer_kernel, out_shape=jax.ShapeDtypeStruct((count, feat)...  70.6 us
    unnamed x9, local copies, waits for them, and re-layouts  5.87 us

profile of v2, /device:TPU:0, one launch (start us, length us, event | category | flops | bytes accessed | tf_op | source)
XLA Modules:
  0.0 78.7 jit_solution(6046110261990989803)
XLA Ops:
  0.0 0.7 broadcast_multiply_fusion
  0.7 0.7 broadcast_add_fusion
  1.3 0.7 slice_bitcast_fusion.2
  2.1 0.1 fusion.table_ref
  2.2 0.0 copy-start
  2.2 1.4 %copy-done = bf16[1,2048,384]{2,1,0:T(8,128)(2,1)S(1)} copy-done((bf16[1,2048,384]{2,1,0:T(8,128)(2,1)S(1)}, bf16[1,2048,384]{2,1,0:T(8,128)(2,1)}, u32[]{:S(2)}) %copy-start) | copy-done | bytes 1572888
  3.6 0.0 copy-start.1
  3.6 1.4 %copy-done.1 = bf16[1,2048,384]{2,1,0:T(8,128)(2,1)S(1)} copy-done((bf16[1,2048,384]{2,1,0:T(8,128)(2,1)S(1)}, bf16[1,2048,384]{2,1,0:T(8,128)(2,1)}, u32[]{:S(2)}) %copy-start.1) | copy-done | bytes 1572888
  5.0 0.0 copy-start.2
  5.0 1.4 %copy-done.2 = bf16[1,384,2048]{2,1,0:T(8,128)(2,1)S(1)} copy-done((bf16[1,384,2048]{2,1,0:T(8,128)(2,1)S(1)}, bf16[1,384,2048]{2,1,0:T(8,128)(2,1)}, u32[]{:S(2)}) %copy-start.2) | copy-done | bytes 1572888
  6.4 0.0 copy-start.3
  6.4 0.9 %copy-done.3 = bf16[64,2048]{1,0:T(8,128)(2,1)S(1)} copy-done((bf16[64,2048]{1,0:T(8,128)(2,1)S(1)}, bf16[64,2048]{1,0:T(8,128)(2,1)}, u32[]{:S(2)}) %copy-start.3) | copy-done | bytes 262168
  7.4 70.6 %shard_map.73 = bf16[64,2048]{1,0:T(8,128)(2,1)S(1)} custom-call(bf16[64,2048]{1,0:T(8,128)(2,1)S(1)} %copy-done.3, bf16[64,128]{1,0:T(8,128)(2,1)S(1)} %fusion.table_ref, bf16[1,2048,384]{2,1,0:T(8,128)(2,1)S(1)} %copy-done, bf16[1,2048,384]{2,1,0:T(8,128)(2,1)S(1)} %copy-done.1, bf16[1,384,2048]{2,1,0:T(8,128)(2,1)S(1)} %copy-done.2), custom_call_target="tpu_custom_call" | custom-call | tf_op jit(solution)/shard_map/pallas_call | solution.py:330
  78.0 0.7 copy.9
  (1 shorter events, 0.0 us)
Async XLA Ops:
  2.2 1.4 %copy-start = (bf16[1,2048,384]{2,1,0:T(8,128)(2,1)S(1)}, bf16[1,2048,384]{2,1,0:T(8,128)(2,1)}, u32[]{:S(2)}) copy-start(bf16[1,2048,384]{2,1,0:T(8,128)(2,1)} %wg_hbm.1) | copy-start | bytes 4718596
  3.6 1.4 %copy-start.1 = (bf16[1,2048,384]{2,1,0:T(8,128)(2,1)S(1)}, bf16[1,2048,384]{2,1,0:T(8,128)(2,1)}, u32[]{:S(2)}) copy-start(bf16[1,2048,384]{2,1,0:T(8,128)(2,1)} %wu_hbm.1) | copy-start | bytes 4718596
  5.0 1.4 %copy-start.2 = (bf16[1,384,2048]{2,1,0:T(8,128)(2,1)S(1)}, bf16[1,384,2048]{2,1,0:T(8,128)(2,1)}, u32[]{:S(2)}) copy-start(bf16[1,384,2048]{2,1,0:T(8,128)(2,1)} %wd_hbm.1) | copy-start | bytes 4718596
  6.4 0.9 %copy-start.3 = (bf16[64,2048]{1,0:T(8,128)(2,1)S(1)}, bf16[64,2048]{1,0:T(8,128)(2,1)}, u32[]{:S(2)}) copy-start(bf16[64,2048]{1,0:T(8,128)(2,1)} %tok_ref.1) | copy-start | bytes 786436

commit v3 on v2

--- a/solution.py
+++ b/solution.py
@@ -98,7 +98,7 @@
 
 
 def layer_kernel(
-    tok_ref, table_ref, wg_hbm, wu_hbm, wd_hbm, out_ref,
+    tok_ref, cid_ref, eid_ref, prob_ref, wg_hbm, wu_hbm, wd_hbm, out_ref,
     rows, part, core_in, x_in, z_in, wg, wu, wd,
     w_sem, zs, zr, xs, xr, ss, sr, ps, pr, bs, br, cs, cr,
 ):
@@ -118,8 +118,6 @@
     ]
     for load in loads:
         load.start()
-    rows[z, pl.ds(0, count), pl.ds(0, feat)] = tok_ref[...]
-    rows[z, pl.ds(0, count), pl.ds(feat, LANES)] = table_ref[...]
 
     barrier = pltpu.get_barrier_semaphore()
     pl.semaphore_signal(barrier, inc=1, device_id=twin, device_id_type=MESH)
@@ -134,6 +132,13 @@
         pl.semaphore_signal(barrier, inc=1, device_id=above, device_id_type=MESH)
 
     middle = (z > 0) & (z < depth - 1)
+    rows[z, pl.ds(0, count), pl.ds(0, feat)] = tok_ref[...]
+    pair = cid_ref[...] * 2 + eid_ref[...]
+    probs = prob_ref[...].astype(jnp.float32)
+    expert = lax.broadcasted_iota(jnp.int32, (LANES, count), 0)
+    table = jnp.where(expert == pair[0:1], probs[0:1], 0.0)
+    table = jnp.where(expert == pair[1:2], probs[1:2], table)
+    rows[z, pl.ds(0, count), pl.ds(feat, LANES)] = table.T.astype(jnp.bfloat16)
     pl.semaphore_wait(barrier, 3 + middle.astype(jnp.int32))
 
     def remote(src, dst, send, recv, device):
@@ -142,60 +147,70 @@
             device_id=device, device_id_type=MESH,
         )
 
-    def block(b, r):
-        return rows.at[b, pl.ds(r * count, count)]
-
-    def piece(b, r):
+    part_rows = count // 2
+
+    def block(b, r, h):
+        return rows.at[b, pl.ds(r * count + h * part_rows, part_rows)]
+
+    def whole(b, r):
         return part.at[b, pl.ds(r * count, count)]
 
-    def to_z(b, up):
-        return remote(block(b, 0), block(b, 0), zs.at[up, b], zr.at[b], above if up else below)
-
-    def to_x(b):
-        return remote(block(b, 0), block(b, 2), xs.at[b], xr.at[b], across)
-
-    def to_twin(b, r):
+    def piece(b, r, h):
+        return part.at[b, pl.ds(r * count + h * part_rows, part_rows)]
+
+    def cut(h):
+        return pl.ds(h * part_rows, part_rows)
+
+    def to_z(b, h, up):
+        near = block(b, 0, h)
+        return remote(near, near, zs.at[up, b, h], zr.at[b, h], above if up else below)
+
+    def to_x(b, h):
+        return remote(block(b, 0, h), block(b, 2, h), xs.at[b, h], xr.at[b, h], across)
+
+    def to_twin(b, r, h):
         i = r // 2
-        return remote(block(b, r), block(b, r + 1), ss.at[i, b], sr.at[i, b], twin)
+        return remote(block(b, r, h), block(b, r + 1, h), ss.at[i, b, h], sr.at[i, b, h], twin)
 
     def part_to_twin(b, r):
         i = r // 2
-        return remote(piece(b, r), core_in.at[i, b], ps.at[i, b], pr.at[i, b], twin)
-
-    def part_to_x(b):
-        return remote(piece(b, 2), x_in.at[b], bs.at[b], br.at[b], across)
-
-    def sum_up(b):
-        return remote(piece(b, 0), z_in.at[b], cs.at[b], cr.at[b], above)
-
-    def sum_down(b):
+        return remote(whole(b, r), core_in.at[i, b], ps.at[i, b], pr.at[i, b], twin)
+
+    def part_to_x(b, h):
+        return remote(piece(b, 2, h), x_in.at[b, cut(h)], bs.at[b, h], br.at[b, h], across)
+
+    def sum_up(b, h):
+        return remote(piece(b, 0, h), z_in.at[b, cut(h)], cs.at[b, h], cr.at[b, h], above)
+
+    def sum_down(b, h):
         last = (b == z - 1).astype(jnp.int32)
         slot = b * (1 - last) + depth * last
-        return remote(piece(b, 0), z_in.at[slot], cs.at[b], cr.at[slot], below)
+        return remote(piece(b, 0, h), z_in.at[slot, cut(h)], cs.at[b, h], cr.at[slot, h], below)
 
     def order(k):
         far = 3 * (2 - z)
         inner = jnp.where(k == 0, z, jnp.where(k == 1, z - 1, jnp.where(k == 2, z + 1, far)))
         return jnp.where(z == 0, k, jnp.where(z == depth - 1, depth - 1 - k, inner))
 
-    def spread(b):
-        to_x(b).start()
-        to_twin(b, 0).start()
-
-    @pl.when(z < depth - 1)
-    def _():
-        to_z(z, 1).start()
-
-    @pl.when(z > 0)
-    def _():
-        to_z(z, 0).start()
-
-    spread(z)
-
-    def fold_core(b):
-        part_to_twin(b, 3).wait_recv()
-        piece(b, 2)[...] = piece(b, 2)[...] + core_in[1, b]
-        part_to_x(b).start()
+    def spread(b, h):
+        to_x(b, h).start()
+        to_twin(b, 0, h).start()
+
+    for h in (0, 1):
+
+        @pl.when(z < depth - 1)
+        def _():
+            to_z(z, h, 1).start()
+
+        @pl.when(z > 0)
+        def _():
+            to_z(z, h, 0).start()
+
+        spread(z, h)
+
+    def fold_core(b, h):
+        piece(b, 2, h)[...] = piece(b, 2, h)[...] + core_in[1, b, cut(h)]
+        part_to_x(b, h).start()
 
     def compute(b):
         lhs = rows[b, :, pl.ds(0, feat)]
@@ -212,105 +227,115 @@
             part[b, :, cols] = (out * weight).astype(jnp.bfloat16)
 
     def stage(d, carry):
-        for side in (-1, 1):
-            b = z + side * d
-
-            @pl.when((d < depth) & (b >= 0) & (b < depth))
-            def _():
-                to_z(b, 0).wait_recv()
-                if side < 0:
-
-                    @pl.when(z < depth - 1)
+        for h in (0, 1):
+            for side in (-1, 1):
+                b = z + side * d
+
+                @pl.when((d < depth) & (b >= 0) & (b < depth))
+                def _():
+                    to_z(b, h, 0).wait_recv()
+
+                    @pl.when((z < depth - 1) if side < 0 else (z > 0))
                     def _():
-                        to_z(b, 1).start()
-                else:
-
-                    @pl.when(z > 0)
-                    def _():
-                        to_z(b, 0).start()
-
-                spread(b)
+                        to_z(b, h, 1 if side < 0 else 0).start()
+
+                    spread(b, h)
 
         b = order(d - 1)
-        to_x(b).wait_recv()
-        to_twin(b, 2).start()
+        for h in (0, 1):
+            to_x(b, h).wait_recv()
+            to_twin(b, 2, h).start()
 
         @pl.when(d == depth)
         def _():
-            fold_core(order(depth - 2))
+            part_to_twin(z, 3).wait_recv()
+            fold_core(z, 0)
 
         @pl.when(d == 1)
         def _():
             for load in loads:
                 load.wait()
 
-        to_twin(b, 0).wait_recv()
-        to_twin(b, 2).wait_recv()
+        for h in (0, 1):
+            to_twin(b, 0, h).wait_recv()
+            to_twin(b, 2, h).wait_recv()
         compute(b)
         part_to_twin(b, 3).start()
         part_to_twin(b, 1).start()
         return carry
 
     lax.fori_loop(1, depth + 1, stage, 0)
-    for k in (3, 1, 0):
-        fold_core(order(k))
-
-    def total(b):
+    for k in (3, 2, 1):
+        part_to_twin(order(k), 3).wait_recv()
+        for h in (0, 1):
+            fold_core(order(k), h)
+    fold_core(z, 1)
+
+    def total(b, h):
+        part_to_x(b, h).wait_recv()
+        value = piece(b, 0, h)[...].astype(jnp.float32)
+        value = value + core_in[0, b, cut(h)].astype(jnp.float32)
+        return value + x_in[b, cut(h)].astype(jnp.float32)
+
+    def fold(j, carry):
+        b = order(depth - 1 - j)
         part_to_twin(b, 1).wait_recv()
-        part_to_x(b).wait_recv()
-        value = piece(b, 0)[...].astype(jnp.float32) + core_in[0, b].astype(jnp.float32)
-        return value + x_in[b].astype(jnp.float32)
-
-    def fold(j, carry):
-        b = order(jnp.where(j == 0, 2, jnp.where(j == 1, 3, 1)))
-        piece(b, 0)[...] = total(b).astype(jnp.bfloat16)
-
-        @pl.when(((b > z) & (z > 0)) | ((b < z) & (z < depth - 1)))
-        def _():
-            sum_up(b).wait_recv()
-            mine = piece(b, 0)[...].astype(jnp.float32)
-            piece(b, 0)[...] = (mine + z_in[b].astype(jnp.float32)).astype(jnp.bfloat16)
-
-        @pl.when(b > z)
-        def _():
-            sum_up(b).start()
-
-        @pl.when(b < z)
-        def _():
-            sum_down(b).start()
+        for h in (0, 1):
+            piece(b, 0, h)[...] = total(b, h).astype(jnp.bfloat16)
+
+            @pl.when(((b > z) & (z > 0)) | ((b < z) & (z < depth - 1)))
+            def _():
+                sum_up(b, h).wait_recv()
+                mine = piece(b, 0, h)[...].astype(jnp.float32)
+                mine = mine + z_in[b, cut(h)].astype(jnp.float32)
+                piece(b, 0, h)[...] = mine.astype(jnp.bfloat16)
+
+            @pl.when(b > z)
+            def _():
+                sum_up(b, h).start()
+
+            @pl.when(b < z)
+            def _():
+                sum_down(b, h).start()
 
         return carry
 
     lax.fori_loop(0, depth - 1, fold, 0)
-    out_ref[...] = total(z).astype(jnp.bfloat16)
-    for slot, there in ((z, z > 0), (depth, z < depth - 1)):
-
-        @pl.when(there)
-        def _():
-            remote(piece(z, 0), z_in.at[slot], cs.at[z], cr.at[slot], across).wait_recv()
-            mine = out_ref[...].astype(jnp.float32)
-            out_ref[...] = (mine + z_in[slot].astype(jnp.float32)).astype(jnp.bfloat16)
+    part_to_twin(z, 1).wait_recv()
+    for h in (0, 1):
+        out_ref[cut(h), :] = total(z, h).astype(jnp.bfloat16)
+        for slot, there in ((z, z > 0), (depth, z < depth - 1)):
+
+            @pl.when(there)
+            def _():
+                inbox = z_in.at[slot, cut(h)]
+                remote(piece(z, 0, h), inbox, cs.at[z, h], cr.at[slot, h], across).wait_recv()
+                mine = out_ref[cut(h), :].astype(jnp.float32)
+                mine = mine + z_in[slot, cut(h)].astype(jnp.float32)
+                out_ref[cut(h), :] = mine.astype(jnp.bfloat16)
 
     def drain(b, carry):
-        @pl.when((z < depth - 1) & (b <= z))
-        def _():
-            to_z(b, 1).wait_send()
-
-        @pl.when((z > 0) & (b >= z))
-        def _():
-            to_z(b, 0).wait_send()
-
-        to_x(b).wait_send()
-        to_twin(b, 0).wait_send()
-        to_twin(b, 2).wait_send()
+        for h in (0, 1):
+
+            @pl.when((z < depth - 1) & (b <= z))
+            def _():
+                to_z(b, h, 1).wait_send()
+
+            @pl.when((z > 0) & (b >= z))
+            def _():
+                to_z(b, h, 0).wait_send()
+
+            to_x(b, h).wait_send()
+            to_twin(b, 0, h).wait_send()
+            to_twin(b, 2, h).wait_send()
+            part_to_x(b, h).wait_send()
+
+            @pl.when(b != z)
+            def _():
+                sum_up(b, h).wait_send()
+
         part_to_twin(b, 1).wait_send()
         part_to_twin(b, 3).wait_send()
-        part_to_x(b).wait_send()
-
-        @pl.when(b != z)
-        def _():
-            sum_up(b).wait_send()
-
         return carry
 
     lax.fori_loop(0, depth, drain, 0)
@@ -319,10 +344,6 @@
 def fused(tokens, cluster_ids, expert_ids, gate_probs, w_gate, w_up, w_down):
     count, feat = tokens.shape
     half = w_gate.shape[2]
-    lane = jnp.arange(LANES)
-    pair = cluster_ids[:, None] * 2 + expert_ids
-    table = jnp.where(pair[:, 0:1] == lane, gate_probs[:, 0:1], 0)
-    table = jnp.where(pair[:, 1:2] == lane, gate_probs[:, 1:2], table).astype(jnp.bfloat16)
     vmem = pl.BlockSpec(memory_space=pltpu.VMEM)
     hbm = pl.BlockSpec(memory_space=pl.ANY)
     b16 = jnp.bfloat16
@@ -330,7 +351,7 @@
     return pl.pallas_call(
         layer_kernel,
         out_shape=jax.ShapeDtypeStruct((count, feat), b16),
-        in_specs=[vmem, vmem, hbm, hbm, hbm],
+        in_specs=[vmem, vmem, vmem, vmem, hbm, hbm, hbm],
         out_specs=vmem,
         scratch_shapes=[
             pltpu.VMEM((4, 4 * count, feat + LANES), b16),
@@ -342,17 +363,17 @@
             pltpu.VMEM((feat, half), b16),
             pltpu.VMEM((half, feat), b16),
             dma((3,)),
-            dma((2, 4)), dma((4,)),
-            dma((4,)), dma((4,)),
+            dma((2, 4, 2)), dma((4, 2)),
+            dma((4, 2)), dma((4, 2)),
+            dma((2, 4, 2)), dma((2, 4, 2)),
             dma((2, 4)), dma((2, 4)),
-            dma((2, 4)), dma((2, 4)),
-            dma((4,)), dma((4,)),
-            dma((4,)), dma((5,)),
+            dma((4, 2)), dma((4, 2)),
+            dma((4, 2)), dma((5, 2)),
         ],
         compiler_params=pltpu.CompilerParams(
-            collective_id=0, has_side_effects=True, vmem_limit_bytes=48 * 2**20
+            collective_id=0, has_side_effects=True, vmem_limit_bytes=62 * 2**20
         ),
-    )(tokens, table, w_gate, w_up, w_down)
+    )(tokens, cluster_ids[None, :], expert_ids.T, gate_probs.T, w_gate, w_up, w_down)
 
 
 def solution(mesh):

time: 79 us -> 62.8 us (0.79)
  Pallas kernels: 70.6 us -> 61 us
  local copies, waits for them, and re-layouts: 6.61 us -> 1.67 us
  other arithmetic: 1.43 us -> 0 us
    pallas_call x1, Pallas kernels: 70.6 us -> 61 us  [fused(): pl.pallas_call(layer_kernel, out_shape=jax.ShapeDtypeStruct((count, feat)...]
    unnamed x9 -> x1, local copies, waits for them, and re-layouts: 5.87 us -> 1.67 us
where the time goes in v3:
time: 62.8 us; the launch traced here: 62.7 us
  Pallas kernels  61 us (97%)
  local copies, waits for them, and re-layouts  1.67 us (3%)
    pallas_call x1, Pallas kernels, fused(): pl.pallas_call(layer_kernel, out_shape=jax.ShapeDtypeStruct((count, feat)...  61 us
    unnamed x1, local copies, waits for them, and re-layouts  1.67 us

profile of v3, /device:TPU:0, one launch (start us, length us, event | category | flops | bytes accessed | tf_op | source)
XLA Modules:
  0.0 62.7 jit_solution(15558495277705884364)
XLA Ops:
  0.0 61.0 %shard_map.73 = bf16[64,2048]{1,0:T(8,128)(2,1)} custom-call(bf16[64,2048]{1,0:T(8,128)(2,1)} %tok_ref.1, s32[1,64]{1,0:T(1,128)} %bitcast.4, s32[2,64]{1,0:T(2,128)} %bitcast.3, bf16[2,64]{1,0:T(2,128)(2,1)} %bitcast.5, bf16[1,2048,384]{2,1,0:T(8,128)(2,1)} %wg_hbm.1, bf16[1,2048,384]{2,1,0:T(8,128)(2,1)} %wu_hbm.1, bf16[1,384,2048]{2,1,0:T(8,128)(2,1)} %wd_hbm.1), custom_call_target="tpu_custom_call" | custom-call | tf_op jit(solution)/shard_map/pallas_call | solution.py:351
  61.0 1.7 %copy.9 = bf16[64,2048]{1,0:T(8,128)(2,1)} copy(bf16[64,2048]{1,0:T(8,128)(2,1)} %shard_map.73) | data formatting | bytes 524288

commit v4 on v3

--- a/solution.py
+++ b/solution.py
@@ -212,19 +212,20 @@
         piece(b, 2, h)[...] = piece(b, 2, h)[...] + core_in[1, b, cut(h)]
         part_to_x(b, h).start()
 
-    def compute(b):
-        lhs = rows[b, :, pl.ds(0, feat)]
+    def compute(b, half):
+        span = pl.ds(half * 2 * count, 2 * count)
+        lhs = rows[b, span, pl.ds(0, feat)]
         gate = jnp.dot(lhs, wg[...], preferred_element_type=jnp.float32)
         up_part = jnp.dot(lhs, wu[...], preferred_element_type=jnp.float32)
         hidden = (gate / (1.0 + jnp.exp(-gate)) * up_part).astype(jnp.bfloat16)
-        weights = rows[b, :, pl.ds(feat, LANES)].astype(jnp.float32)
+        weights = rows[b, span, pl.ds(feat, LANES)].astype(jnp.float32)
         lane = lax.broadcasted_iota(jnp.int32, weights.shape, 1)
         weight = jnp.sum(jnp.where(lane == own_expert, weights, 0.0), axis=1, keepdims=True)
         tile = min(feat, 512)
         for n in range(feat // tile):
             cols = pl.ds(n * tile, tile)
             out = jnp.dot(hidden, wd[:, cols], preferred_element_type=jnp.float32)
-            part[b, :, cols] = (out * weight).astype(jnp.bfloat16)
+            part[b, span, cols] = (out * weight).astype(jnp.bfloat16)
 
     def stage(d, carry):
         for h in (0, 1):
@@ -242,6 +243,16 @@
                     spread(b, h)
 
         b = order(d - 1)
+
+        @pl.when(d == 1)
+        def _():
+            for load in loads:
+                load.wait()
+
+        for h in (0, 1):
+            to_twin(b, 0, h).wait_recv()
+        compute(b, 0)
+        part_to_twin(b, 1).start()
         for h in (0, 1):
             to_x(b, h).wait_recv()
             to_twin(b, 2, h).start()
@@ -251,17 +262,10 @@
             part_to_twin(z, 3).wait_recv()
             fold_core(z, 0)
 
-        @pl.when(d == 1)
-        def _():
-            for load in loads:
-                load.wait()
-
-        for h in (0, 1):
-            to_twin(b, 0, h).wait_recv()
+        for h in (0, 1):
             to_twin(b, 2, h).wait_recv()
-        compute(b)
+        compute(b, 1)
         part_to_twin(b, 3).start()
-        part_to_twin(b, 1).start()
         return carry
 
     lax.fori_loop(1, depth + 1, stage, 0)

time: 62.8 us -> 62.5 us (level)
  no operation moved by 1% of the time
where the time goes in v4:
time: 62.5 us; the launch traced here: 62.4 us
  Pallas kernels  60.7 us (97%)
  local copies, waits for them, and re-layouts  1.67 us (3%)
    pallas_call x1, Pallas kernels, fused(): pl.pallas_call(layer_kernel, out_shape=jax.ShapeDtypeStruct((count, feat)...  60.7 us
    unnamed x1, local copies, waits for them, and re-layouts  1.67 us

profile of v4, /device:TPU:0, one launch (start us, length us, event | category | flops | bytes accessed | tf_op | source)
XLA Modules:
  0.0 62.4 jit_solution(9688119810434390690)
XLA Ops:
  0.0 60.7 %shard_map.73 = bf16[64,2048]{1,0:T(8,128)(2,1)} custom-call(bf16[64,2048]{1,0:T(8,128)(2,1)} %tok_ref.1, s32[1,64]{1,0:T(1,128)} %bitcast.4, s32[2,64]{1,0:T(2,128)} %bitcast.3, bf16[2,64]{1,0:T(2,128)(2,1)} %bitcast.5, bf16[1,2048,384]{2,1,0:T(8,128)(2,1)} %wg_hbm.1, bf16[1,2048,384]{2,1,0:T(8,128)(2,1)} %wu_hbm.1, bf16[1,384,2048]{2,1,0:T(8,128)(2,1)} %wd_hbm.1), custom_call_target="tpu_custom_call" | custom-call | tf_op jit(solution)/shard_map/pallas_call | solution.py:355
  60.7 1.7 %copy.9 = bf16[64,2048]{1,0:T(8,128)(2,1)} copy(bf16[64,2048]{1,0:T(8,128)(2,1)} %shard_map.73) | data formatting | bytes 524288
